TPU v7x, 32 devices: a whole 2x2x4 slice. The times are simulated.
32 devices in a mesh: seq: 8 (over y, x, core), head: 4 (over z).
Axes of the slice: x: 2, y: 2, z: 4, core: 2. Of those that a mesh axis runs over, the one named last changes fastest.
Arguments:
- tokens: bfloat16 [8192, 512], P(('seq', 'head')), may hold values from -6 to 6
- w_proj: bfloat16 [512, 2048], replicated, may hold values from -0.25 to 0.25
- w_out: bfloat16 [512, 512], replicated, may hold values from -0.25 to 0.25
- tile_user: int32 [64], replicated, may hold values from 0 to 15, never falling along the last dimension, each value on 1 to 40 neighbouring positions
Outputs:
- mixed: bfloat16 [8192, 512], P(('seq', 'head'))
Inputs may be any that keep to these rules, and one draw needn't show every extreme that they name: `tile_user`: tile users never fall along the tiles; each user covers 1 to 40 tiles, one exactly 40; every number of 0 to 15 occurs.
All inputs are finite; a program needn't handle non-finite values.
Results may differ from a plain program's by a relative error of at most 0.0052.
Values may be sent and summed in bfloat16 or wider, within the bound.
No kernel may reach another device: no remote copies, remote signals or barrier semaphores. Data moves between devices by JAX's collectives and lax.ppermute only.
A program may use at most 128 MiB of HBM per device.

v0:
```python
import functools

import jax
import jax.numpy as jnp
from jax import lax
from jax.experimental import pallas as pl
from jax.experimental.pallas import tpu as pltpu
from jax.sharding import PartitionSpec as P

H = 8
DH = 64
TILE = 128
LANES = 2 * DH
TEAM = H // 2

epsilon = 1e-05

f32 = jnp.float32
bf16 = jnp.bfloat16


def layer_norm(values):
    center = values - jnp.mean(values, axis=-1, keepdims=True)
    spread = jnp.mean(center * center, axis=-1, keepdims=True)
    return center * lax.rsqrt(spread + epsilon)


def silu(values):
    half = values * 0.5
    return half + half * jnp.tanh(half)


def swap_halves(values):
    return pltpu.roll(values, DH, 1)


def low_lanes(rows):
    return lax.broadcasted_iota(jnp.int32, (rows, LANES), 1) < DH


def project(me_ref, tokens_ref, weights_ref, *refs):
    outs, (tokens, weights, held, sems) = refs[:-4], refs[-4:]
    rows = tokens.shape[0]
    half = rows // 2
    copies = [[pltpu.make_async_copy(tokens_ref, tokens, sems.at[0])]]
    deep = weights.shape[1] // 2
    for i, block in enumerate((3, 1, 2)):
        pieces = []
        for j in range(2):
            inner = pl.ds(j * deep, deep)
            source = weights_ref.at[inner, pl.ds(block * H * DH, H * DH)]
            pieces.append(
                pltpu.make_async_copy(source, weights.at[i, inner], sems.at[1 + 2 * i + j])
            )
        copies.append(pieces)
    for pieces in copies:
        for copy in pieces:
            copy.start()

    def wait(number):
        for copy in copies[number]:
            copy.wait()

    wait(0)
    normed = layer_norm(tokens[...].astype(f32)).astype(bf16)
    low, half_low = low_lanes(rows), low_lanes(half)
    scale = 0.5 * DH ** (-0.5)
    wait(1)
    keys = silu(jnp.dot(normed, weights[0], preferred_element_type=f32))
    wait(2)
    values = silu(jnp.dot(normed, weights[1], preferred_element_type=f32))
    for pair in range(H // 2):
        at = slice(pair * LANES, (pair + 1) * LANES)
        key, value = keys[:, at], values[:, at]
        held[2 * pair, :rows] = jnp.where(low, key, swap_halves(value)).astype(bf16)
        held[2 * pair + 1, :rows] = jnp.where(low, swap_halves(key), value).astype(bf16)
    wait(3)
    queries = silu(jnp.dot(normed, weights[2], preferred_element_type=f32)) * scale
    for pair in range(H // 2):
        at = slice(pair * LANES, (pair + 1) * LANES)
        upper, lower = queries[:half, at], queries[half:, at]
        held[2 * pair, rows:] = jnp.where(half_low, upper, swap_halves(lower)).astype(bf16)
        held[2 * pair + 1, rows:] = jnp.where(half_low, swap_halves(upper), lower).astype(bf16)
    for k, out in enumerate(outs):
        out[...] = held[jnp.bitwise_xor(me_ref[0], k)]


def project_gating(tokens_ref, weights_ref, out_ref, tokens, weights, sems):
    copies = [
        pltpu.make_async_copy(tokens_ref, tokens, sems.at[0]),
        pltpu.make_async_copy(weights_ref.at[:, pl.ds(0, H * DH)], weights, sems.at[1]),
    ]
    for copy in copies:
        copy.start()
    for copy in copies:
        copy.wait()
    normed = layer_norm(tokens[...].astype(f32)).astype(bf16)
    gating = silu(jnp.dot(normed, weights[...], preferred_element_type=f32))
    out_ref[...] = gating.astype(bf16)


def attend(
    start_ref, inverse_ref, block_ref, team_ref, slot_ref, out_team, queries_ref, held, *refs
):
    step = pl.program_id(0)
    *before, out_ref, total, queries = refs
    rows = held.shape[1]
    half = rows // 2
    tiles = rows // TILE
    low = low_lanes(half)
    blocks = [block_ref[step * TEAM + i] for i in range(TEAM)]
    for i in range(TEAM):
        packed = queries_ref[i].astype(f32)
        queries[i * rows : i * rows + half] = jnp.where(low, packed, 0.0).astype(bf16)
        queries[i * rows + half : (i + 1) * rows] = jnp.where(
            low, swap_halves(packed), 0.0
        ).astype(bf16)
    starts = [start_ref[block * tiles + j] for block in blocks for j in range(tiles)]
    least, low_start, high_start, high_first = blocks[0], starts[0], starts[0], starts[0]
    for block in blocks[1:]:
        least = jnp.minimum(least, block)
    for start in starts[1:]:
        low_start = jnp.minimum(low_start, start)
        high_start = jnp.maximum(high_start, start)
    for start in starts[tiles::tiles]:
        high_first = jnp.maximum(high_first, start)
    total[...] = jnp.zeros_like(total)

    def add(team, key_block, masked, chosen):
        key_rows = jnp.concatenate([held[slot_ref[team * TEAM + i]] for i in range(TEAM)], axis=0)
        if masked:
            column = lax.broadcasted_iota(jnp.int32, (TILE, TEAM * rows), 1)
            ahead = column - lax.broadcasted_iota(jnp.int32, (TILE, TEAM * rows), 0)

        def add_to(i, count=1):
            at = slice(i * rows, (i + count) * rows)
            score = lax.dot_general(
                queries[at], key_rows, (((1,), (1,)), ((), ())), preferred_element_type=f32
            )
            weights = score + score * jnp.tanh(score)
            if masked:
                pieces = []
                for j in range(tiles):
                    from_start = starts[i * tiles + j] * TILE - key_block * rows
                    to_row = (blocks[i] - key_block) * rows + j * TILE
                    allowed = (column >= from_start) & (ahead <= to_row)
                    pieces.append(jnp.where(allowed, weights[j * TILE : (j + 1) * TILE], 0.0))
                weights = jnp.concatenate(pieces, axis=0)
            total[at] += jnp.dot(weights.astype(bf16), key_rows, preferred_element_type=f32)

        if not masked:
            for i in range(0, TEAM, 2):
                add_to(i, 2)
            return
        for i in range(TEAM):
            if chosen:
                needed = starts[i * tiles] < (key_block + TEAM) * tiles
                pl.when(needed)(functools.partial(add_to, i))
            else:
                add_to(i)

    def add_diagonal(team):
        key_rows = jnp.concatenate([held[slot_ref[team * TEAM + i]] for i in range(TEAM)], axis=0)
        turn = blocks[0] - least
        for i in range(TEAM):
            seen = (i + 1) * rows
            at = pl.ds(pl.multiple_of(jnp.bitwise_xor(turn, i) * rows, rows), rows)
            score = lax.dot_general(
                queries[at], key_rows[:seen], (((1,), (1,)), ((), ())), preferred_element_type=f32
            )
            weights = score + score * jnp.tanh(score)
            column = lax.broadcasted_iota(jnp.int32, (TILE, seen), 1)
            ahead = column - lax.broadcasted_iota(jnp.int32, (TILE, seen), 0)
            pieces = []
            for j in range(tiles):
                from_start = start_ref[(least + i) * tiles + j] * TILE - least * rows
                allowed = (column >= from_start) & (ahead <= i * rows + j * TILE)
                pieces.append(jnp.where(allowed, weights[j * TILE : (j + 1) * TILE], 0.0))
            weights = jnp.concatenate(pieces, axis=0).astype(bf16)
            total[at] += jnp.dot(weights, key_rows[:seen], preferred_element_type=f32)

    def one_team(team, carry):
        key_block = team_ref[team]
        earlier = (key_block < least) & ((key_block + TEAM) * tiles > low_start)
        whole = key_block * tiles >= high_start
        every = (key_block + TEAM) * tiles > high_first
        pl.when(earlier & whole)(lambda: add(team, key_block, False, False))
        pl.when(earlier & ~every)(lambda: add(team, key_block, True, True))
        pl.when(earlier & ~whole & every)(lambda: add(team, key_block, True, False))
        pl.when(key_block == least)(lambda: add_diagonal(team))
        return carry

    lax.fori_loop(0, held.shape[0] // TEAM, one_team, 0)
    for i in range(TEAM):
        at = i * rows
        upper = total[at : at + half] * inverse_ref[blocks[i] * tiles]
        lower = total[at + half : at + rows] * inverse_ref[blocks[i] * tiles + tiles - 1]
        packed = jnp.where(low, swap_halves(upper), lower)
        for more in before:
            packed = packed + more[blocks[i] - least].astype(f32)
        out_ref[blocks[i] - least] = packed.astype(out_ref.dtype)


def attend_call(tables, queries, keys, gives, *before):
    half, rows = queries.shape[1], 2 * queries.shape[1]
    steps = queries.shape[0] // TEAM
    packed = pl.BlockSpec((TEAM, half, LANES), lambda i, *_: (i, 0, 0))
    placed = pl.BlockSpec((TEAM, half, LANES), lambda i, *refs: (refs[5][i], 0, 0))
    return pl.pallas_call(
        attend,
        grid_spec=pltpu.PrefetchScalarGridSpec(
            num_scalar_prefetch=6,
            grid=(steps,),
            in_specs=[
                packed,
                pl.BlockSpec(keys.shape, lambda i, *_: (0, 0, 0), pipeline_mode=pl.Buffered(1)),
            ]
            + [placed] * len(before),
            out_specs=placed,
            scratch_shapes=[
                pltpu.VMEM((TEAM * rows, LANES), f32),
                pltpu.VMEM((TEAM * rows, LANES), bf16),
            ],
        ),
        out_shape=jax.ShapeDtypeStruct(queries.shape, gives),
        compiler_params=pltpu.CompilerParams(vmem_limit_bytes=24 << 20),
        cost_estimate=pl.CostEstimate(
            flops=steps * 2_000_000_000, bytes_accessed=4_000_000, transcendentals=4_000_000
        ),
        name="attend",
    )(*tables, queries, keys, *before)


def finish(tokens_ref, attention_ref, gating_ref, weights_ref, out_ref):
    rows = tokens_ref.shape[0]
    half = rows // 2
    low = low_lanes(half)
    uppers, lowers = [], []
    for pair in range(H // 2):
        one = attention_ref[2 * pair].astype(f32)
        two = attention_ref[2 * pair + 1].astype(f32)
        uppers.append(jnp.where(low, one, swap_halves(two)))
        lowers.append(jnp.where(low, swap_halves(one), two))
    attention = jnp.concatenate(
        [jnp.concatenate(uppers, axis=1), jnp.concatenate(lowers, axis=1)], axis=0
    )
    gated = (layer_norm(attention) * gating_ref[...].astype(f32)).astype(bf16)
    mixed = tokens_ref[...].astype(f32) + jnp.dot(
        gated, weights_ref[...], preferred_element_type=f32
    )
    out_ref[...] = mixed.astype(bf16)


VMEM = pl.BlockSpec(memory_space=pltpu.VMEM)
SMEM = pl.BlockSpec(memory_space=pltpu.SMEM)
HBM = pl.BlockSpec(memory_space=pltpu.HBM)


def per_device(seq_size, head_size, tokens, w_proj, w_out, tile_user):
    rows, width = tokens.shape
    half = rows // 2
    tiles = rows // TILE
    blocks = seq_size * head_size
    seq, head = lax.axis_index("seq"), lax.axis_index("head")
    fold = H // head_size
    share = fold
    groups = seq_size // (fold * share)
    group, part, core = seq // (fold * share), (seq // share) % fold, seq % share
    me = part * head_size + head
    me_array = me.reshape(1).astype(jnp.int32)

    def partner(array, k):
        if k == 0:
            return array
        pairs = []
        for s in range(seq_size):
            for h in range(head_size):
                g, p, c = s // (fold * share), (s // share) % fold, s % share
                other = (p * head_size + h) ^ k
                t = (g * fold + other // head_size) * share + c
                pairs.append((s * head_size + h, t * head_size + other % head_size))
        return lax.ppermute(array, ("seq", "head"), pairs)

    def seq_flip(array, bit):
        return lax.ppermute(array, "seq", [(s, s ^ bit) for s in range(seq_size)])

    sent = pl.pallas_call(
        project,
        out_shape=[jax.ShapeDtypeStruct((rows + half, LANES), bf16)] * H,
        in_specs=[SMEM, HBM, HBM],
        out_specs=[VMEM] * H,
        scratch_shapes=[
            pltpu.VMEM((rows, width), bf16),
            pltpu.VMEM((3, width, H * DH), bf16),
            pltpu.VMEM((H, rows + half, LANES), bf16),
            pltpu.SemaphoreType.DMA((7,)),
        ],
        compiler_params=pltpu.CompilerParams(vmem_limit_bytes=53 << 20),
        name="project",
    )(me_array, tokens, w_proj)
    def gating_of(tokens):
        return pl.pallas_call(
            project_gating,
            out_shape=jax.ShapeDtypeStruct((rows, H * DH), bf16),
            in_specs=[HBM, HBM],
            out_specs=VMEM,
            scratch_shapes=[
                pltpu.VMEM((rows, width), bf16),
                pltpu.VMEM((width, H * DH), bf16),
                pltpu.SemaphoreType.DMA((2,)),
            ],
            compiler_params=pltpu.CompilerParams(vmem_limit_bytes=12 << 20),
            name="project_gating",
        )(tokens, w_proj)

    start = jnp.sum((tile_user[None, :] < tile_user[:, None]).astype(jnp.int32), axis=1)
    length = jnp.sum((tile_user[None, :] == tile_user[:, None]).astype(f32), axis=1) * TILE
    asked = jnp.arange(H, dtype=jnp.int32) ^ me

    def blocks_of(places, in_group, in_core):
        in_seq = (in_group * fold + places // head_size) * share + in_core
        return in_seq * head_size + places % head_size

    order = [0, 1, 5, 4, 2, 3, 6, 7]
    place_of = jnp.array([order.index(k) for k in range(H)], jnp.int32)
    arrived = {0: sent[0]}
    for k in order[1:-2]:
        arrived[k] = partner(sent[k], k)
    first_lot = jnp.stack([arrived[k][:rows] for k in order[:TEAM]])
    *held_back, first_lot = lax.optimization_barrier((sent[order[-2]], sent[order[-1]], first_lot))
    for k, array in zip(order[-2:], held_back):
        arrived[k] = partner(array, k)
    queries = jnp.stack([arrived[k][rows:] for k in range(H)])
    lots = [first_lot, jnp.stack([arrived[k][:rows] for k in order[TEAM:]])]
    keys = jnp.concatenate(lots)
    first_places = jnp.arange(0, H, TEAM, dtype=jnp.int32)
    mine = blocks_of(asked, group, core)
    out_team = asked[::TEAM] // TEAM
    if groups == 2 and share == 2:
        far_keys = jnp.concatenate([seq_flip(lot, fold * share) for lot in lots])
        other_queries = seq_flip(queries, 1)
        others = blocks_of(asked, group, 1 - core)

        def tables(query_blocks, in_group):
            teams = blocks_of(first_places, in_group, core)
            return start, 1.0 / length, query_blocks, teams, place_of[asked], out_team

        near_ours = attend_call(tables(mine, group), queries, keys, f32)
        near_theirs = attend_call(tables(others, group), other_queries, keys, f32)
        gating = gating_of(lax.optimization_barrier((tokens, near_theirs))[0])
        far_keys, near_theirs, near_ours, gating = lax.optimization_barrier(
            (far_keys, near_theirs, near_ours, gating)
        )
        theirs = attend_call(
            tables(others, 1 - group), other_queries, far_keys, bf16, near_theirs
        )
        theirs = seq_flip(theirs, 1)
        ours = attend_call(tables(mine, 1 - group), queries, far_keys, f32, near_ours)
        attention = (ours + theirs.astype(f32)).astype(bf16)
    else:
        everything = lax.all_gather(keys, "seq", axis=0, tiled=True)
        index = jnp.arange(blocks, dtype=jnp.int32)
        slot = index // head_size * H + place_of[jnp.bitwise_xor(index % head_size, me)]
        tables = (start, 1.0 / length, mine, index[::TEAM], slot, out_team)
        attention = attend_call(tables, queries, everything, bf16)
        gating = gating_of(tokens)
    teams = [
        [
            ((g * fold + p) * share + c) * head_size + h
            for p in range(fold)
            for h in range(head_size)
        ]
        for g in range(groups)
        for c in range(share)
    ]
    returned = lax.all_to_all(
        attention, ("seq", "head"), 0, 0, axis_index_groups=teams, tiled=True
    )
    return pl.pallas_call(
        finish,
        out_shape=jax.ShapeDtypeStruct((rows, width), bf16),
        in_specs=[VMEM, VMEM, VMEM, VMEM],
        out_specs=VMEM,
        compiler_params=pltpu.CompilerParams(vmem_limit_bytes=12 << 20),
        name="finish",
    )(tokens, returned, gating, w_out)


def solution(mesh):
    placed = (P(("seq", "head"), None), P(), P(), P())
    return jax.shard_map(
        functools.partial(per_device, mesh.shape["seq"], mesh.shape["head"]),
        mesh=mesh,
        in_specs=placed,
        out_specs=P(("seq", "head"), None),
        check_vma=False,
    )
```

profile of v0, /device:TPU:4, one launch (start us, length us, event | category | flops | bytes accessed | tf_op | source)
XLA Modules:
  0.0 61.9 jit_solution(340613434042799580)
XLA Ops:
  0.0 2.6 %project.1 = (bf16[384,128]{1,0:T(8,128)(2,1)S(1)}, bf16[384,128]{1,0:T(8,128)(2,1)S(1)}, bf16[384,128]{1,0:T(8,128)(2,1)S(1)}, bf16[384,128]{1,0:T(8,128)(2,1)S...) custom-call(s32[1]{0:T(128)} %bitcast.1.me_ref, ...), custom_call_target="tpu_custom_call" | custom-call | tf_op jit(solution)/shard_map/project/pallas_call | solution.py:287
  2.6 1.6 %collective-permute-start = (bf16[384,128]{1,0:T(8,128)(2,1)S(1)}, bf16[384,128]{1,0:T(8,128)(2,1)S(1)}, u32[]{:S(2)}, u32[]{:S(2)}) collective-permute-start(bf16[384,128]{1,0:T(8,128)(2,1)S(1)} %get-tuple-element.22), channel_id=1, source_target_pairs={{0,1},{1,0},{2,3},{3,2},{4,5},{5,4},{6,7},{7,6},{8,9},{9,8},{10,11... | collective-permute-start | bytes 294920 | tf_op jit(solution)/shard_map/ppermute | solution.py:282
  4.2 2.6 %collective-permute-start.1 = (bf16[384,128]{1,0:T(8,128)(2,1)S(1)}, bf16[384,128]{1,0:T(8,128)(2,1)S(1)}, u32[]{:S(2)}, u32[]{:S(2)}) collective-permute-start(bf16[384,128]{1,0:T(8,128)(2,1)S(1)} %get-tuple-element.23), channel_id=1, source_target_pairs={{0,2},{1,3},{2,0},{3,1},{4,6},{5,7},{6,4},{7,5},{8,10},{9,11},{10,... | collective-permute-start | bytes 294920 | tf_op jit(solution)/shard_map/ppermute | solution.py:282
  6.8 0.2 collective-permute-start.2
  7.0 1.5 %collective-permute-start.3 = (bf16[384,128]{1,0:T(8,128)(2,1)S(1)}, bf16[384,128]{1,0:T(8,128)(2,1)S(1)}, u32[]{:S(2)}, u32[]{:S(2)}) collective-permute-start(bf16[384,128]{1,0:T(8,128)(2,1)S(1)} %get-tuple-element.25), channel_id=1, source_target_pairs={{0,8},{1,9},{2,10},{3,11},{4,12},{5,13},{6,14},{7,15},{8,0},{9,1},... | collective-permute-start | bytes 294920 | tf_op jit(solution)/shard_map/ppermute | solution.py:282
  8.5 0.6 %collective-permute-start.4 = (bf16[384,128]{1,0:T(8,128)(2,1)S(1)}, bf16[384,128]{1,0:T(8,128)(2,1)S(1)}, u32[]{:S(2)}, u32[]{:S(2)}) collective-permute-start(bf16[384,128]{1,0:T(8,128)(2,1)S(1)} %get-tuple-element.26), channel_id=1, source_target_pairs={{0,9},{1,8},{2,11},{3,10},{4,13},{5,12},{6,15},{7,14},{8,1},{9,0},... | collective-permute-start | bytes 294920 | tf_op jit(solution)/shard_map/ppermute | solution.py:282
  9.2 0.2 convert_reduce_fusion.1.start_ref
  9.4 0.2 convert_reduce_fusion
  9.8 0.6 %gather_fusion = s32[8]{0:T(128)S(1)} fusion(s32[8]{0:T(128)S(1)} %copy-done.3, s32[1024]{0:T(1024)S(1)} %pad_clamp_fusion), kind=kCustom, calls=%fused_computation | custom fusion | bytes 96 | tf_op jit(solution)/shard_map/gather | solution.py:346
  10.5 2.2 %collective-permute-done.3 = bf16[384,128]{1,0:T(8,128)(2,1)S(1)} collective-permute-done((bf16[384,128]{1,0:T(8,128)(2,1)S(1)}, bf16[384,128]{1,0:T(8,128)(2,1)S(1)}, u32[]{:S(2)}, u32[]{:S(2)}) %collective-permute-start.3) | collective-permute-done | bytes 98336 | tf_op jit(solution)/shard_map/ppermute | solution.py:282
  12.7 3.3 %collective-permute-done.4 = bf16[384,128]{1,0:T(8,128)(2,1)S(1)} collective-permute-done((bf16[384,128]{1,0:T(8,128)(2,1)S(1)}, bf16[384,128]{1,0:T(8,128)(2,1)S(1)}, u32[]{:S(2)}, u32[]{:S(2)}) %collective-permute-start.4) | collective-permute-done | bytes 98336 | tf_op jit(solution)/shard_map/ppermute | solution.py:282
  16.1 1.0 %collective-permute-start.5 = (bf16[384,128]{1,0:T(8,128)(2,1)S(1)}, bf16[384,128]{1,0:T(8,128)(2,1)S(1)}, u32[]{:S(2)}, u32[]{:S(2)}) collective-permute-start(bf16[384,128]{1,0:T(8,128)(2,1)S(1)} %get-tuple-element.29), channel_id=1, source_target_pairs={{0,10},{1,11},{2,8},{3,9},{4,14},{5,15},{6,12},{7,13},{8,2},{9,3},... | collective-permute-start | bytes 294920 | tf_op jit(solution)/shard_map/ppermute | solution.py:282
  17.1 2.5 %collective-permute-start.6 = (bf16[384,128]{1,0:T(8,128)(2,1)S(1)}, bf16[384,128]{1,0:T(8,128)(2,1)S(1)}, u32[]{:S(2)}, u32[]{:S(2)}) collective-permute-start(bf16[384,128]{1,0:T(8,128)(2,1)S(1)} %get-tuple-element.30), channel_id=1, source_target_pairs={{0,11},{1,10},{2,9},{3,8},{4,15},{5,14},{6,13},{7,12},{8,3},{9,2},... | collective-permute-start | bytes 294920 | tf_op jit(solution)/shard_map/ppermute | solution.py:282
  19.6 0.5 collective-permute-start.7
  20.3 5.4 %collective-permute-done.5 = bf16[384,128]{1,0:T(8,128)(2,1)S(1)} collective-permute-done((bf16[384,128]{1,0:T(8,128)(2,1)S(1)}, bf16[384,128]{1,0:T(8,128)(2,1)S(1)}, u32[]{:S(2)}, u32[]{:S(2)}) %collective-permute-start.5) | collective-permute-done | bytes 98336 | tf_op jit(solution)/shard_map/ppermute | solution.py:282
  25.9 0.6 collective-permute-start.8
  26.5 5.2 %attend.5.refs_0_ = f32[8,128,128]{2,1,0:T(8,128)S(1)} custom-call(s32[64]{0:T(128)S(1)} %convert_reduce_fusion.1.start_ref, f32[64]{0:T(128)S(1)} %multiply_divide_fusion.inverse_ref, s32[8]{0:T(128)S(1)} %get-tuple-element.38.block_ref, s32[2]{0:T(128)S(1)} %get-tuple-element.40.team_ref, s32[8]{0:T(128)S(1)} %gather_fusion, ...), custom_call_target="tpu_custom_call" | custom-call | flops 4000000000 | bytes 4000000 | tf_op jit(solution)/shard_map/attend/pallas_call | solution.py:209
  31.8 2.5 %attend.4.refs_0_ = f32[8,128,128]{2,1,0:T(8,128)S(1)} custom-call(s32[64]{0:T(128)S(1)} %convert_reduce_fusion.1.start_ref, f32[64]{0:T(128)S(1)} %multiply_divide_fusion.inverse_ref, s32[8]{0:T(128)S(1)} %get-tuple-element.37.block_ref, s32[2]{0:T(128)S(1)} %get-tuple-element.40.team_ref, s32[8]{0:T(128)S(1)} %gather_fusion, ...), custom_call_target="tpu_custom_call" | custom-call | flops 4000000000 | bytes 4000000 | tf_op jit(solution)/shard_map/attend/pallas_call | solution.py:209
  34.3 0.6 %project_gating.1.gating_ref = bf16[256,512]{1,0:T(8,128)(2,1)S(1)} custom-call(bf16[256,512]{1,0:T(8,128)(2,1)S(1)} %copy-done.1, bf16[512,2048]{1,0:T(8,128)(2,1)S(1)} %copy-done), custom_call_target="tpu_custom_call" | custom-call | tf_op jit(solution)/shard_map/project_gating/pallas_call | solution.py:302
  35.1 2.8 %attend.7 = bf16[8,128,128]{2,1,0:T(8,128)(2,1)S(1)} custom-call(s32[64]{0:T(128)S(1)} %convert_reduce_fusion.1.start_ref, f32[64]{0:T(128)S(1)} %multiply_divide_fusion.inverse_ref, s32[8]{0:T(128)S(1)} %get-tuple-element.37.block_ref, s32[2]{0:T(128)S(1)} %multiply_add_fusion.2.team_ref, s32[8]{0:T(128)S(1)} %gather_fusion, ...), custom_call_target="tpu_custom_call" | custom-call | flops 4000000000 | bytes 4000000 | tf_op jit(solution)/shard_map/attend/pallas_call | solution.py:209
  37.8 4.2 %collective-permute-start.10 = (bf16[8,128,128]{2,1,0:T(8,128)(2,1)S(1)}, bf16[8,128,128]{2,1,0:T(8,128)(2,1)S(1)}, u32[]{:S(2)}, u32[]{:S(2)}) collective-permute-start(bf16[8,128,128]{2,1,0:T(8,128)(2,1)S(1)} %attend.7), channel_id=1, source_target_pairs={{0,4},{4,0},{8,12},{12,8},{16,20},{20,16},{24,28},{28,24},{1,5},{5... | collective-permute-start | bytes 786440 | tf_op jit(solution)/shard_map/ppermute | solution.py:285
  42.0 4.1 %attend.6 = f32[8,128,128]{2,1,0:T(8,128)S(1)} custom-call(s32[64]{0:T(128)S(1)} %convert_reduce_fusion.1.start_ref, f32[64]{0:T(128)S(1)} %multiply_divide_fusion.inverse_ref, s32[8]{0:T(128)S(1)} %get-tuple-element.38.block_ref, s32[2]{0:T(128)S(1)} %multiply_add_fusion.2.team_ref, s32[8]{0:T(128)S(1)} %gather_fusion, s32[2]{0:T(128)S(1)} %get-tuple-element.39.out_team, ...), custom_call_target="tpu_custom_call" | custom-call | flops 4000000000 | bytes 4000000 | tf_op jit(solution)/shard_map/attend/pallas_call | solution.py:209
  46.2 14.3 %all_to_all.5.attention_ref = bf16[8,128,128]{2,1,0:T(8,128)(2,1)S(1)} all-to-all(bf16[8,128,128]{2,1,0:T(8,128)(2,1)S(1)} %add_convert_fusion), channel_id=1, replica_groups={{0,1,2,3,8,9,10,11},{4,5,6,7,12,13,14,15},{16,17,18,19,24,25,26,27},{20..., dimensions={0} | all-to-all | bytes 524288 | tf_op jit(solution)/shard_map/all_to_all | solution.py:376
  60.5 1.4 %finish.1 = bf16[256,512]{1,0:T(8,128)(2,1)} custom-call(bf16[256,512]{1,0:T(8,128)(2,1)S(1)} %copy-done.1, bf16[8,128,128]{2,1,0:T(8,128)(2,1)S(1)} %all_to_all.5.attention_ref, bf16[256,512]{1,0:T(8,128)(2,1)S(1)} %project_gating.1.gating_ref, bf16[512,512]{1,0:T(8,128)(2,1)S(1)} %copy-done.2), custom_call_target="tpu_custom_call" | custom-call | tf_op jit(solution)/shard_map/finish/pallas_call | solution.py:379
  (52 shorter events, 0.7 us)
Async XLA Ops:
  0.0 9.8 %copy-start.3 = (s32[8]{0:T(128)S(1)}, s32[8]{0:T(128)}, u32[]{:S(2)}) copy-start(s32[8]{0:T(128)} %constant.129.clone) | copy-start | bytes 100
  0.0 9.2 %copy-start.4 = (s32[64]{0:T(128)S(1)}, s32[64]{0:T(128)}, u32[]{:S(2)}) copy-start(s32[64]{0:T(128)} %param.8) | copy-start | bytes 772
  2.6 7.9 %collective-permute-start = (bf16[384,128]{1,0:T(8,128)(2,1)S(1)}, bf16[384,128]{1,0:T(8,128)(2,1)S(1)}, u32[]{:S(2)}, u32[]{:S(2)}) collective-permute-start(bf16[384,128]{1,0:T(8,128)(2,1)S(1)} %get-tuple-element.22), channel_id=1, source_target_pairs={{0,1},{1,0},{2,3},{3,2},{4,5},{5,4},{6,7},{7,6},{8,9},{9,8},{10,11... | collective-permute-start | bytes 294920 | tf_op jit(solution)/shard_map/ppermute | solution.py:282
  4.2 15.9 %collective-permute-start.1 = (bf16[384,128]{1,0:T(8,128)(2,1)S(1)}, bf16[384,128]{1,0:T(8,128)(2,1)S(1)}, u32[]{:S(2)}, u32[]{:S(2)}) collective-permute-start(bf16[384,128]{1,0:T(8,128)(2,1)S(1)} %get-tuple-element.23), channel_id=1, source_target_pairs={{0,2},{1,3},{2,0},{3,1},{4,6},{5,7},{6,4},{7,5},{8,10},{9,11},{10,... | collective-permute-start | bytes 294920 | tf_op jit(solution)/shard_map/ppermute | solution.py:282
  6.8 13.4 %collective-permute-start.2 = (bf16[384,128]{1,0:T(8,128)(2,1)S(1)}, bf16[384,128]{1,0:T(8,128)(2,1)S(1)}, u32[]{:S(2)}, u32[]{:S(2)}) collective-permute-start(bf16[384,128]{1,0:T(8,128)(2,1)S(1)} %get-tuple-element.24), channel_id=1, source_target_pairs={{0,3},{1,2},{2,1},{3,0},{4,7},{5,6},{6,5},{7,4},{8,11},{9,10},{10,... | collective-permute-start | bytes 294920 | tf_op jit(solution)/shard_map/ppermute | solution.py:282
  7.0 5.7 %collective-permute-start.3 = (bf16[384,128]{1,0:T(8,128)(2,1)S(1)}, bf16[384,128]{1,0:T(8,128)(2,1)S(1)}, u32[]{:S(2)}, u32[]{:S(2)}) collective-permute-start(bf16[384,128]{1,0:T(8,128)(2,1)S(1)} %get-tuple-element.25), channel_id=1, source_target_pairs={{0,8},{1,9},{2,10},{3,11},{4,12},{5,13},{6,14},{7,15},{8,0},{9,1},... | collective-permute-start | bytes 294920 | tf_op jit(solution)/shard_map/ppermute | solution.py:282
  8.5 7.5 %collective-permute-start.4 = (bf16[384,128]{1,0:T(8,128)(2,1)S(1)}, bf16[384,128]{1,0:T(8,128)(2,1)S(1)}, u32[]{:S(2)}, u32[]{:S(2)}) collective-permute-start(bf16[384,128]{1,0:T(8,128)(2,1)S(1)} %get-tuple-element.26), channel_id=1, source_target_pairs={{0,9},{1,8},{2,11},{3,10},{4,13},{5,12},{6,15},{7,14},{8,1},{9,0},... | collective-permute-start | bytes 294920 | tf_op jit(solution)/shard_map/ppermute | solution.py:282
  16.1 9.6 %collective-permute-start.5 = (bf16[384,128]{1,0:T(8,128)(2,1)S(1)}, bf16[384,128]{1,0:T(8,128)(2,1)S(1)}, u32[]{:S(2)}, u32[]{:S(2)}) collective-permute-start(bf16[384,128]{1,0:T(8,128)(2,1)S(1)} %get-tuple-element.29), channel_id=1, source_target_pairs={{0,10},{1,11},{2,8},{3,9},{4,14},{5,15},{6,12},{7,13},{8,2},{9,3},... | collective-permute-start | bytes 294920 | tf_op jit(solution)/shard_map/ppermute | solution.py:282
  17.1 8.7 %collective-permute-start.6 = (bf16[384,128]{1,0:T(8,128)(2,1)S(1)}, bf16[384,128]{1,0:T(8,128)(2,1)S(1)}, u32[]{:S(2)}, u32[]{:S(2)}) collective-permute-start(bf16[384,128]{1,0:T(8,128)(2,1)S(1)} %get-tuple-element.30), channel_id=1, source_target_pairs={{0,11},{1,10},{2,9},{3,8},{4,15},{5,14},{6,13},{7,12},{8,3},{9,2},... | collective-permute-start | bytes 294920 | tf_op jit(solution)/shard_map/ppermute | solution.py:282
  19.6 15.3 %collective-permute-start.7 = (bf16[4,256,128]{2,1,0:T(8,128)(2,1)S(1)}, bf16[4,256,128]{2,1,0:T(8,128)(2,1)S(1)}, u32[]{:S(2)}, u32[]{:S(2)}) collective-permute-start(bf16[4,256,128]{2,1,0:T(8,128)(2,1)S(1)} %pad_maximum_fusion.1), channel_id=1, source_target_pairs={{0,16},{4,20},{8,24},{12,28},{16,0},{20,4},{24,8},{28,12},{1,17},{... | collective-permute-start | bytes 786440 | tf_op jit(solution)/shard_map/ppermute | solution.py:285
  25.8 6.0 %collective-permute-start.9 = (bf16[8,128,128]{2,1,0:T(8,128)(2,1)S(1)}, bf16[8,128,128]{2,1,0:T(8,128)(2,1)S(1)}, u32[]{:S(2)}, u32[]{:S(2)}) collective-permute-start(bf16[8,128,128]{2,1,0:T(8,128)(2,1)S(1)} %fusion.queries_ref), channel_id=1, source_target_pairs={{0,4},{4,0},{8,12},{12,8},{16,20},{20,16},{24,28},{28,24},{1,5},{5... | collective-permute-start | bytes 786440 | tf_op jit(solution)/shard_map/ppermute | solution.py:285
  25.9 9.1 %collective-permute-start.8 = (bf16[4,256,128]{2,1,0:T(8,128)(2,1)S(1)}, bf16[4,256,128]{2,1,0:T(8,128)(2,1)S(1)}, u32[]{:S(2)}, u32[]{:S(2)}) collective-permute-start(bf16[4,256,128]{2,1,0:T(8,128)(2,1)S(1)} %pad_maximum_fusion.2), channel_id=1, source_target_pairs={{0,16},{4,20},{8,24},{12,28},{16,0},{20,4},{24,8},{28,12},{1,17},{... | collective-permute-start | bytes 786440 | tf_op jit(solution)/shard_map/ppermute | solution.py:285
  31.8 2.6 %copy-start = (bf16[512,2048]{1,0:T(8,128)(2,1)S(1)}, bf16[512,2048]{1,0:T(8,128)(2,1)}, u32[]{:S(2)}) copy-start(bf16[512,2048]{1,0:T(8,128)(2,1)} %weights_ref.4) | copy-start | bytes 6291460
  31.8 2.6 %copy-start.1 = (bf16[256,512]{1,0:T(8,128)(2,1)S(1)}, bf16[256,512]{1,0:T(8,128)(2,1)}, u32[]{:S(2)}) copy-start(bf16[256,512]{1,0:T(8,128)(2,1)} %tokens_ref.4) | copy-start | bytes 786436
  37.8 22.7 %copy-start.2 = (bf16[512,512]{1,0:T(8,128)(2,1)S(1)}, bf16[512,512]{1,0:T(8,128)(2,1)}, u32[]{:S(2)}) copy-start(bf16[512,512]{1,0:T(8,128)(2,1)} %weights_ref.5) | copy-start | bytes 1572868
  37.8 8.3 %collective-permute-start.10 = (bf16[8,128,128]{2,1,0:T(8,128)(2,1)S(1)}, bf16[8,128,128]{2,1,0:T(8,128)(2,1)S(1)}, u32[]{:S(2)}, u32[]{:S(2)}) collective-permute-start(bf16[8,128,128]{2,1,0:T(8,128)(2,1)S(1)} %attend.7), channel_id=1, source_target_pairs={{0,4},{4,0},{8,12},{12,8},{16,20},{20,16},{24,28},{28,24},{1,5},{5... | collective-permute-start | bytes 786440 | tf_op jit(solution)/shard_map/ppermute | solution.py:285
where the time goes:
time: 62 us; the launch traced here: 61.9 us
  Pallas kernels  19.2 us (31%)
  starting transfers between devices  15.4 us (25%)
  blocking collectives  14.3 us (23%)
  waiting for transfers between devices  11 us (18%)
  local copies, waits for them, and re-layouts  0.96 us (2%)
    pallas_call x4, Pallas kernels, attend_call(): pl.pallas_call(attend, grid_spec=pltpu.PrefetchScalarGridSpec(num_scalar_...  14.6 us
    all_to_all x1, blocking collectives, per_device(): lax.all_to_all(attention, ('seq', 'head'), 0, 0, axis_index_groups=teams,...  14.3 us
    ppermute x7, waiting for transfers between devices, partner(): return lax.ppermute(array, ('seq', 'head'), pairs)  11 us
    ppermute x7, starting transfers between devices, partner(): return lax.ppermute(array, ('seq', 'head'), pairs)  10.1 us
    ppermute x4, starting transfers between devices, seq_flip(): return lax.ppermute(array, 'seq', [(s, s ^ bit) for s in range(seq_size)])  5.32 us
    pallas_call x1, Pallas kernels, per_device(): pl.pallas_call(project, out_shape=[jax.ShapeDtypeStruct((rows + half, LAN...  2.58 us
    pallas_call x1, Pallas kernels, per_device(): pl.pallas_call(finish, out_shape=jax.ShapeDtypeStruct((rows, width), bf16...  1.39 us
  transfers between devices with their start and end apart: 11, of which 3 were waited for; matrix products, arithmetic and copies ran while one was open for 2% of the time, Pallas kernels for 20%

commit v1 on v0

--- a/solution.py
+++ b/solution.py
@@ -351,11 +351,18 @@
         far_keys, near_theirs, near_ours, gating = lax.optimization_barrier(
             (far_keys, near_theirs, near_ours, gating)
         )
-        theirs = attend_call(
-            tables(others, 1 - group), other_queries, far_keys, bf16, near_theirs
-        )
-        theirs = seq_flip(theirs, 1)
-        ours = attend_call(tables(mine, 1 - group), queries, far_keys, f32, near_ours)
+
+        def add_far(queries, query_blocks, sums, gives):
+            return lax.cond(
+                group > 0,
+                lambda: attend_call(
+                    tables(query_blocks, 1 - group), queries, far_keys, gives, sums
+                ),
+                lambda: sums.astype(gives),
+            )
+
+        theirs = seq_flip(add_far(other_queries, others, near_theirs, bf16), 1)
+        ours = add_far(queries, mine, near_ours, f32)
         attention = (ours + theirs.astype(f32)).astype(bf16)
     else:
         everything = lax.all_gather(keys, "seq", axis=0, tiled=True)

time: 62 us -> 63.5 us (1.024)
  waiting for transfers between devices: 11 us -> 9.41 us
  starting transfers between devices: 15.4 us -> 16.8 us
  local copies, waits for them, and re-layouts: 0.96 us -> 2.27 us
    ppermute x7, starting transfers between devices: 10.1 us -> 12.1 us  [partner(): return lax.ppermute(array, ('seq', 'head'), pairs)]
    ppermute x7, waiting for transfers between devices: 11 us -> 9.4 us  [partner(): return lax.ppermute(array, ('seq', 'head'), pairs)]
    gather x1 -> x3, local copies, waits for them, and re-layouts: 0.64 us -> 1.93 us  [tables(): return (start, 1.0 / length, query_blocks, teams, place_of[asked], out_team)]
  transfers between devices with their start and end apart: 11 -> 11, of which waited for: 3 -> 4; matrix products, arithmetic and copies ran while one was open for 2% -> 3% of each run, Pallas kernels for 20% -> 20%
where the time goes in v1:
time: 63.5 us; the launch traced here: 63.3 us
  Pallas kernels  19.5 us (31%)
  starting transfers between devices  16.8 us (26%)
  blocking collectives  14 us (22%)
  waiting for transfers between devices  9.41 us (15%)
  local copies, waits for them, and re-layouts  2.27 us (4%)
  other arithmetic  0.65 us (1%)
    pallas_call x4, Pallas kernels, attend_call(): pl.pallas_call(attend, grid_spec=pltpu.PrefetchScalarGridSpec(num_scalar_...  14.9 us
    all_to_all x1, blocking collectives, per_device(): lax.all_to_all(attention, ('seq', 'head'), 0, 0, axis_index_groups=teams,...  14 us
    ppermute x7, starting transfers between devices, partner(): return lax.ppermute(array, ('seq', 'head'), pairs)  12.1 us
    ppermute x7, waiting for transfers between devices, partner(): return lax.ppermute(array, ('seq', 'head'), pairs)  9.4 us
    ppermute x4, starting transfers between devices, seq_flip(): return lax.ppermute(array, 'seq', [(s, s ^ bit) for s in range(seq_size)])  4.73 us
    pallas_call x1, Pallas kernels, per_device(): pl.pallas_call(project, out_shape=[jax.ShapeDtypeStruct((rows + half, LAN...  2.58 us
    gather x3, local copies, waits for them, and re-layouts, tables(): return (start, 1.0 / length, query_blocks, teams, place_of[asked], out_team)  1.93 us
    pallas_call x1, Pallas kernels, per_device(): pl.pallas_call(finish, out_shape=jax.ShapeDtypeStruct((rows, width), bf16...  1.38 us
  transfers between devices with their start and end apart: 11, of which 4 were waited for; matrix products, arithmetic and copies ran while one was open for 3% of the time, Pallas kernels for 20%

profile of v1, /device:TPU:4, one launch (start us, length us, event | category | flops | bytes accessed | tf_op | source)
XLA Modules:
  0.0 63.3 jit_solution(12078825520541462805)
XLA Ops:
  0.0 2.6 %project.1 = (bf16[384,128]{1,0:T(8,128)(2,1)S(1)}, bf16[384,128]{1,0:T(8,128)(2,1)S(1)}, bf16[384,128]{1,0:T(8,128)(2,1)S(1)}, bf16[384,128]{1,0:T(8,128)(2,1)S...) custom-call(s32[1]{0:T(128)} %bitcast.me_ref, ...), custom_call_target="tpu_custom_call" | custom-call | tf_op jit(solution)/shard_map/project/pallas_call | solution.py:287
  2.6 1.6 %collective-permute-start.2 = (bf16[384,128]{1,0:T(8,128)(2,1)S(1)}, bf16[384,128]{1,0:T(8,128)(2,1)S(1)}, u32[]{:S(2)}, u32[]{:S(2)}) collective-permute-start(bf16[384,128]{1,0:T(8,128)(2,1)S(1)} %get-tuple-element.110), channel_id=1, source_target_pairs={{0,8},{1,9},{2,10},{3,11},{4,12},{5,13},{6,14},{7,15},{8,0},{9,1},... | collective-permute-start | bytes 294920 | tf_op jit(solution)/shard_map/ppermute | solution.py:282
  4.1 1.5 %collective-permute-start.1 = (bf16[384,128]{1,0:T(8,128)(2,1)S(1)}, bf16[384,128]{1,0:T(8,128)(2,1)S(1)}, u32[]{:S(2)}, u32[]{:S(2)}) collective-permute-start(bf16[384,128]{1,0:T(8,128)(2,1)S(1)} %get-tuple-element.109), channel_id=1, source_target_pairs={{0,9},{1,8},{2,11},{3,10},{4,13},{5,12},{6,15},{7,14},{8,1},{9,0},... | collective-permute-start | bytes 294920 | tf_op jit(solution)/shard_map/ppermute | solution.py:282
  6.1 2.6 %collective-permute-start.4 = (bf16[384,128]{1,0:T(8,128)(2,1)S(1)}, bf16[384,128]{1,0:T(8,128)(2,1)S(1)}, u32[]{:S(2)}, u32[]{:S(2)}) collective-permute-start(bf16[384,128]{1,0:T(8,128)(2,1)S(1)} %get-tuple-element.112), channel_id=1, source_target_pairs={{0,2},{1,3},{2,0},{3,1},{4,6},{5,7},{6,4},{7,5},{8,10},{9,11},{10,... | collective-permute-start | bytes 294920 | tf_op jit(solution)/shard_map/ppermute | solution.py:282
  8.7 1.3 %collective-permute-start.5 = (bf16[384,128]{1,0:T(8,128)(2,1)S(1)}, bf16[384,128]{1,0:T(8,128)(2,1)S(1)}, u32[]{:S(2)}, u32[]{:S(2)}) collective-permute-start(bf16[384,128]{1,0:T(8,128)(2,1)S(1)} %get-tuple-element.113), channel_id=1, source_target_pairs={{0,3},{1,2},{2,1},{3,0},{4,7},{5,6},{6,5},{7,4},{8,11},{9,10},{10,... | collective-permute-start | bytes 294920 | tf_op jit(solution)/shard_map/ppermute | solution.py:282
  10.7 0.6 %gather_fusion.2 = s32[8]{0:T(128)S(1)} fusion(s32[8]{0:T(128)S(1)} %copy-done.3, s32[1024]{0:T(1024)S(1)} %pad_clamp_fusion.2), kind=kCustom, calls=%fused_computation.2 | custom fusion | bytes 96 | tf_op jit(solution)/shard_map/gather | solution.py:346
  11.4 0.8 %collective-permute-done.1 = bf16[384,128]{1,0:T(8,128)(2,1)S(1)} collective-permute-done((bf16[384,128]{1,0:T(8,128)(2,1)S(1)}, bf16[384,128]{1,0:T(8,128)(2,1)S(1)}, u32[]{:S(2)}, u32[]{:S(2)}) %collective-permute-start.1) | collective-permute-done | bytes 98336 | tf_op jit(solution)/shard_map/ppermute | solution.py:282
  12.1 0.6 collective-permute-done
  12.8 2.7 %collective-permute-start.6 = (bf16[384,128]{1,0:T(8,128)(2,1)S(1)}, bf16[384,128]{1,0:T(8,128)(2,1)S(1)}, u32[]{:S(2)}, u32[]{:S(2)}) collective-permute-start(bf16[384,128]{1,0:T(8,128)(2,1)S(1)} %get-tuple-element.114), channel_id=1, source_target_pairs={{0,10},{1,11},{2,8},{3,9},{4,14},{5,15},{6,12},{7,13},{8,2},{9,3},... | collective-permute-start | bytes 294920 | tf_op jit(solution)/shard_map/ppermute | solution.py:282
  15.5 1.9 %collective-permute-start.7 = (bf16[384,128]{1,0:T(8,128)(2,1)S(1)}, bf16[384,128]{1,0:T(8,128)(2,1)S(1)}, u32[]{:S(2)}, u32[]{:S(2)}) collective-permute-start(bf16[384,128]{1,0:T(8,128)(2,1)S(1)} %get-tuple-element.115), channel_id=1, source_target_pairs={{0,11},{1,10},{2,9},{3,8},{4,15},{5,14},{6,13},{7,12},{8,3},{9,2},... | collective-permute-start | bytes 294920 | tf_op jit(solution)/shard_map/ppermute | solution.py:282
  18.3 7.7 %collective-permute-done.6 = bf16[384,128]{1,0:T(8,128)(2,1)S(1)} collective-permute-done((bf16[384,128]{1,0:T(8,128)(2,1)S(1)}, bf16[384,128]{1,0:T(8,128)(2,1)S(1)}, u32[]{:S(2)}, u32[]{:S(2)}) %collective-permute-start.6) | collective-permute-done | bytes 98336 | tf_op jit(solution)/shard_map/ppermute | solution.py:282
  26.3 0.6 collective-permute-start.8
  26.9 5.2 %attend.7 = f32[8,128,128]{2,1,0:T(8,128)S(1)} custom-call(s32[64]{0:T(128)S(1)} %convert_reduce_fusion.1.start_ref, f32[64]{0:T(128)S(1)} %get-tuple-element.122.inverse_ref, s32[8]{0:T(128)S(1)} %get-tuple-element.123.block_ref, s32[2]{0:T(128)S(1)} %get-tuple-element.126.team_ref, s32[8]{0:T(128)S(1)} %gather_fusion.2, s32[2]{0:T(128)S(1)} %get-tuple-element.125.out_team, ...), custom_call_target="tpu_custom_call" | custom-call | flops 4000000000 | bytes 4000000 | tf_op jit(solution)/shard_map/attend/pallas_call | solution.py:209
  32.1 3.1 %attend.6 = f32[8,128,128]{2,1,0:T(8,128)S(1)} custom-call(s32[64]{0:T(128)S(1)} %convert_reduce_fusion.1.start_ref, f32[64]{0:T(128)S(1)} %get-tuple-element.122.inverse_ref, s32[8]{0:T(128)S(1)} %get-tuple-element.124.block_ref, s32[2]{0:T(128)S(1)} %get-tuple-element.126.team_ref, s32[8]{0:T(128)S(1)} %gather_fusion.2, s32[2]{0:T(128)S(1)} %get-tuple-element.125.out_team, ...), custom_call_target="tpu_custom_call" | custom-call | flops 4000000000 | bytes 4000000 | tf_op jit(solution)/shard_map/attend/pallas_call | solution.py:209
  35.2 0.6 project_gating.1.gating_ref
  35.9 3.5 %conditional.3 = (bf16[8,128,128]{2,1,0:T(8,128)(2,1)S(1)}) conditional(s32[]{:T(128)} %convert_element_type.19, f32[8,128,128]{2,1,0:T(8,128)S(1)} %attend.6, (f32[64]{0:T(128)S(1)}, s32[]{:T(128)}, s32[2]{0:T(128)S(1)}, s32[2]{0:T(128)S(1)}, s32[]{:T(128)}, /*index=5*/s32[8]{0:T(128)S(1)}, s32[8]{0:T(128)S(1)}, s32[64]{0:T(128)S(1)}, ...), branch_computations={%region_4.5_spmd, %region_5.6_spmd} | conditional | flops 4000001280 | bytes 4004864 | solution.py:356
  36.0 0.6 %gather_fusion.1 = s32[8]{0:T(128)S(1)} fusion(s32[8]{0:T(128)S(1)} %get-tuple-element.83, s32[1024]{0:T(1024)S(1)} %pad_clamp_fusion.1), kind=kCustom, calls=%fused_computation.1 | custom fusion | bytes 96 | tf_op jit(solution)/shard_map/cond/branch_1_fun/gather | solution.py:346
  36.6 2.5 %attend.5 = bf16[8,128,128]{2,1,0:T(8,128)(2,1)S(1)} custom-call(s32[64]{0:T(128)S(1)} %get-tuple-element.76.start_ref, f32[64]{0:T(128)S(1)} %broadcast_divide_fusion.1.inverse_ref, s32[8]{0:T(128)S(1)} %get-tuple-element.78.block_ref, s32[2]{0:T(128)S(1)} %fusion.2.team_ref, s32[8]{0:T(128)S(1)} %gather_fusion.1, s32[2]{0:T(128)S(1)} %get-tuple-element.85.out_team, ...), custom_call_target="tpu_custom_call" | custom-call | flops 4000000000 | bytes 4000000 | tf_op jit(solution)/shard_map/cond/branch_1_fun/attend/pallas_call | solution.py:209
  39.4 3.6 %collective-permute-start.10 = (bf16[8,128,128]{2,1,0:T(8,128)(2,1)S(1)}, bf16[8,128,128]{2,1,0:T(8,128)(2,1)S(1)}, u32[]{:S(2)}, u32[]{:S(2)}) collective-permute-start(bf16[8,128,128]{2,1,0:T(8,128)(2,1)S(1)} %get-tuple-element.128), channel_id=1, source_target_pairs={{0,4},{4,0},{8,12},{12,8},{16,20},{20,16},{24,28},{28,24},{1,5},{5... | collective-permute-start | bytes 786440 | tf_op jit(solution)/shard_map/ppermute | solution.py:285
  43.0 4.8 %conditional.2 = (f32[8,128,128]{2,1,0:T(8,128)S(1)}) conditional(s32[]{:T(128)} %convert_element_type.19, f32[8,128,128]{2,1,0:T(8,128)S(1)} %attend.7, (f32[64]{0:T(128)S(1)}, s32[]{:T(128)}, s32[2]{0:T(128)S(1)}, s32[2]{0:T(128)S(1)}, s32[]{:T(128)}, /*index=5*/s32[8]{0:T(128)S(1)}, s32[8]{0:T(128)S(1)}, s32[64]{0:T(128)S(1)}, s32[8]{0:T(128)S(1)}, ...), branch_computations={%region_2.3_spmd, %region_3.4_spmd} | conditional | flops 4000001280 | bytes 5053440 | solution.py:356
  43.0 0.6 %gather_fusion = s32[8]{0:T(128)S(1)} fusion(s32[8]{0:T(128)S(1)} %get-tuple-element.70, s32[1024]{0:T(1024)S(1)} %pad_clamp_fusion), kind=kCustom, calls=%fused_computation | custom fusion | bytes 96 | tf_op jit(solution)/shard_map/cond/branch_1_fun/gather | solution.py:346
  43.7 4.1 %attend.4 = f32[8,128,128]{2,1,0:T(8,128)S(1)} custom-call(s32[64]{0:T(128)S(1)} %get-tuple-element.62.start_ref, f32[64]{0:T(128)S(1)} %broadcast_divide_fusion.inverse_ref, s32[8]{0:T(128)S(1)} %get-tuple-element.65.block_ref, s32[2]{0:T(128)S(1)} %fusion.team_ref, s32[8]{0:T(128)S(1)} %gather_fusion, s32[2]{0:T(128)S(1)} %get-tuple-element.72.out_team, ...), custom_call_target="tpu_custom_call" | custom-call | flops 4000000000 | bytes 4000000 | tf_op jit(solution)/shard_map/cond/branch_1_fun/attend/pallas_call | solution.py:209
  47.9 14.0 %all_to_all.5.attention_ref = bf16[8,128,128]{2,1,0:T(8,128)(2,1)S(1)} all-to-all(bf16[8,128,128]{2,1,0:T(8,128)(2,1)S(1)} %add_convert_fusion), channel_id=1, replica_groups={{0,1,2,3,8,9,10,11},{4,5,6,7,12,13,14,15},{16,17,18,19,24,25,26,27},{20..., dimensions={0} | all-to-all | bytes 524288 | tf_op jit(solution)/shard_map/all_to_all | solution.py:383
  61.9 1.4 %finish.1 = bf16[256,512]{1,0:T(8,128)(2,1)} custom-call(bf16[256,512]{1,0:T(8,128)(2,1)S(1)} %copy-done.1, bf16[8,128,128]{2,1,0:T(8,128)(2,1)S(1)} %all_to_all.5.attention_ref, bf16[256,512]{1,0:T(8,128)(2,1)S(1)} %project_gating.1.gating_ref, bf16[512,512]{1,0:T(8,128)(2,1)S(1)} %copy-done.2), custom_call_target="tpu_custom_call" | custom-call | tf_op jit(solution)/shard_map/finish/pallas_call | solution.py:386
  (65 shorter events, 2.3 us)
Async XLA Ops:
  0.0 10.7 %copy-start.3 = (s32[8]{0:T(128)S(1)}, s32[8]{0:T(128)}, u32[]{:S(2)}) copy-start(s32[8]{0:T(128)} %constant.183.clone) | copy-start | bytes 100
  0.0 10.1 %copy-start.4 = (s32[64]{0:T(128)S(1)}, s32[64]{0:T(128)}, u32[]{:S(2)}) copy-start(s32[64]{0:T(128)} %param.12) | copy-start | bytes 772
  2.6 8.8 %collective-permute-start.2 = (bf16[384,128]{1,0:T(8,128)(2,1)S(1)}, bf16[384,128]{1,0:T(8,128)(2,1)S(1)}, u32[]{:S(2)}, u32[]{:S(2)}) collective-permute-start(bf16[384,128]{1,0:T(8,128)(2,1)S(1)} %get-tuple-element.110), channel_id=1, source_target_pairs={{0,8},{1,9},{2,10},{3,11},{4,12},{5,13},{6,14},{7,15},{8,0},{9,1},... | collective-permute-start | bytes 294920 | tf_op jit(solution)/shard_map/ppermute | solution.py:282
  4.1 8.0 %collective-permute-start.1 = (bf16[384,128]{1,0:T(8,128)(2,1)S(1)}, bf16[384,128]{1,0:T(8,128)(2,1)S(1)}, u32[]{:S(2)}, u32[]{:S(2)}) collective-permute-start(bf16[384,128]{1,0:T(8,128)(2,1)S(1)} %get-tuple-element.109), channel_id=1, source_target_pairs={{0,9},{1,8},{2,11},{3,10},{4,13},{5,12},{6,15},{7,14},{8,1},{9,0},... | collective-permute-start | bytes 294920 | tf_op jit(solution)/shard_map/ppermute | solution.py:282
  5.7 7.0 %collective-permute-start = (bf16[384,128]{1,0:T(8,128)(2,1)S(1)}, bf16[384,128]{1,0:T(8,128)(2,1)S(1)}, u32[]{:S(2)}, u32[]{:S(2)}) collective-permute-start(bf16[384,128]{1,0:T(8,128)(2,1)S(1)} %get-tuple-element.108), channel_id=1, source_target_pairs={{0,1},{1,0},{2,3},{3,2},{4,5},{5,4},{6,7},{7,6},{8,9},{9,8},{10,11... | collective-permute-start | bytes 294920 | tf_op jit(solution)/shard_map/ppermute | solution.py:282
  6.1 11.8 %collective-permute-start.4 = (bf16[384,128]{1,0:T(8,128)(2,1)S(1)}, bf16[384,128]{1,0:T(8,128)(2,1)S(1)}, u32[]{:S(2)}, u32[]{:S(2)}) collective-permute-start(bf16[384,128]{1,0:T(8,128)(2,1)S(1)} %get-tuple-element.112), channel_id=1, source_target_pairs={{0,2},{1,3},{2,0},{3,1},{4,6},{5,7},{6,4},{7,5},{8,10},{9,11},{10,... | collective-permute-start | bytes 294920 | tf_op jit(solution)/shard_map/ppermute | solution.py:282
  8.7 9.5 %collective-permute-start.5 = (bf16[384,128]{1,0:T(8,128)(2,1)S(1)}, bf16[384,128]{1,0:T(8,128)(2,1)S(1)}, u32[]{:S(2)}, u32[]{:S(2)}) collective-permute-start(bf16[384,128]{1,0:T(8,128)(2,1)S(1)} %get-tuple-element.113), channel_id=1, source_target_pairs={{0,3},{1,2},{2,1},{3,0},{4,7},{5,6},{6,5},{7,4},{8,11},{9,10},{10,... | collective-permute-start | bytes 294920 | tf_op jit(solution)/shard_map/ppermute | solution.py:282
  12.8 13.3 %collective-permute-start.6 = (bf16[384,128]{1,0:T(8,128)(2,1)S(1)}, bf16[384,128]{1,0:T(8,128)(2,1)S(1)}, u32[]{:S(2)}, u32[]{:S(2)}) collective-permute-start(bf16[384,128]{1,0:T(8,128)(2,1)S(1)} %get-tuple-element.114), channel_id=1, source_target_pairs={{0,10},{1,11},{2,8},{3,9},{4,14},{5,15},{6,12},{7,13},{8,2},{9,3},... | collective-permute-start | bytes 294920 | tf_op jit(solution)/shard_map/ppermute | solution.py:282
  15.5 10.6 %collective-permute-start.7 = (bf16[384,128]{1,0:T(8,128)(2,1)S(1)}, bf16[384,128]{1,0:T(8,128)(2,1)S(1)}, u32[]{:S(2)}, u32[]{:S(2)}) collective-permute-start(bf16[384,128]{1,0:T(8,128)(2,1)S(1)} %get-tuple-element.115), channel_id=1, source_target_pairs={{0,11},{1,10},{2,9},{3,8},{4,15},{5,14},{6,13},{7,12},{8,3},{9,2},... | collective-permute-start | bytes 294920 | tf_op jit(solution)/shard_map/ppermute | solution.py:282
  17.4 18.4 %collective-permute-start.3 = (bf16[4,256,128]{2,1,0:T(8,128)(2,1)S(1)}, bf16[4,256,128]{2,1,0:T(8,128)(2,1)S(1)}, u32[]{:S(2)}, u32[]{:S(2)}) collective-permute-start(bf16[4,256,128]{2,1,0:T(8,128)(2,1)S(1)} %pad_maximum_fusion.1), channel_id=1, source_target_pairs={{0,16},{4,20},{8,24},{12,28},{16,0},{20,4},{24,8},{28,12},{1,17},{... | collective-permute-start | bytes 786440 | tf_op jit(solution)/shard_map/ppermute | solution.py:285
  26.1 5.9 %collective-permute-start.9 = (bf16[8,128,128]{2,1,0:T(8,128)(2,1)S(1)}, bf16[8,128,128]{2,1,0:T(8,128)(2,1)S(1)}, u32[]{:S(2)}, u32[]{:S(2)}) collective-permute-start(bf16[8,128,128]{2,1,0:T(8,128)(2,1)S(1)} %fusion.4.queries_ref), channel_id=1, source_target_pairs={{0,4},{4,0},{8,12},{12,8},{16,20},{20,16},{24,28},{28,24},{1,5},{5... | collective-permute-start | bytes 786440 | tf_op jit(solution)/shard_map/ppermute | solution.py:285
  26.3 9.6 %collective-permute-start.8 = (bf16[4,256,128]{2,1,0:T(8,128)(2,1)S(1)}, bf16[4,256,128]{2,1,0:T(8,128)(2,1)S(1)}, u32[]{:S(2)}, u32[]{:S(2)}) collective-permute-start(bf16[4,256,128]{2,1,0:T(8,128)(2,1)S(1)} %pad_maximum_fusion.2), channel_id=1, source_target_pairs={{0,16},{4,20},{8,24},{12,28},{16,0},{20,4},{24,8},{28,12},{1,17},{... | collective-permute-start | bytes 786440 | tf_op jit(solution)/shard_map/ppermute | solution.py:285
  32.1 3.1 %copy-start = (bf16[512,2048]{1,0:T(8,128)(2,1)S(1)}, bf16[512,2048]{1,0:T(8,128)(2,1)}, u32[]{:S(2)}) copy-start(bf16[512,2048]{1,0:T(8,128)(2,1)} %weights_ref.4) | copy-start | bytes 6291460
  32.1 3.1 %copy-start.1 = (bf16[256,512]{1,0:T(8,128)(2,1)S(1)}, bf16[256,512]{1,0:T(8,128)(2,1)}, u32[]{:S(2)}) copy-start(bf16[256,512]{1,0:T(8,128)(2,1)} %tokens_ref.4) | copy-start | bytes 786436
  39.4 8.4 %collective-permute-start.10 = (bf16[8,128,128]{2,1,0:T(8,128)(2,1)S(1)}, bf16[8,128,128]{2,1,0:T(8,128)(2,1)S(1)}, u32[]{:S(2)}, u32[]{:S(2)}) collective-permute-start(bf16[8,128,128]{2,1,0:T(8,128)(2,1)S(1)} %get-tuple-element.128), channel_id=1, source_target_pairs={{0,4},{4,0},{8,12},{12,8},{16,20},{20,16},{24,28},{28,24},{1,5},{5... | collective-permute-start | bytes 786440 | tf_op jit(solution)/shard_map/ppermute | solution.py:285
  43.0 18.9 %copy-start.2 = (bf16[512,512]{1,0:T(8,128)(2,1)S(1)}, bf16[512,512]{1,0:T(8,128)(2,1)}, u32[]{:S(2)}) copy-start(bf16[512,512]{1,0:T(8,128)(2,1)} %weights_ref.5) | copy-start | bytes 1572868
